TPU v7x, 32 devices: a whole 2x2x4 slice. The times are simulated.
32 devices in a mesh: pipe: 4 (over z), expert: 8 (over y, x, core).
Axes of the slice: x: 2, y: 2, z: 4, core: 2. Of those that a mesh axis runs over, the one named last changes fastest.
Arguments:
- forward_input: bfloat16 [4, 1024, 2048], P('pipe', 'expert'), may hold values from -6 to 6
- queries: bfloat16 [4, 1024, 2048], P('pipe', 'expert'), may hold values from -100 to 100
- new_keys: bfloat16 [4, 1024, 256], P('pipe', 'expert'), may hold values from -6 to 6
- new_values: bfloat16 [4, 1024, 256], P('pipe', 'expert'), may hold values from -6 to 6
- cache_keys: bfloat16 [4, 1024, 256], P('pipe', 'expert'), may hold values from -6 to 6
- cache_values: bfloat16 [4, 1024, 256], P('pipe', 'expert'), may hold values from -6 to 6
- context_lengths: int32 [4, 8], P('pipe', 'expert'), may hold values from 1 to 128
- norm_gain: float32 [4, 2048], P('pipe'), may hold values from 0.5 to 1.5
- router: bfloat16 [4, 2048, 8], P('pipe'), may hold values from -0.125 to 0.125
- gate_weight: bfloat16 [4, 8, 2048, 768], P('pipe', 'expert'), may hold values from -0.125 to 0.125
- up_weight: bfloat16 [4, 8, 2048, 768], P('pipe', 'expert'), may hold values from -0.125 to 0.125
- down_weight: bfloat16 [4, 8, 768, 2048], P('pipe', 'expert'), may hold values from -0.21875 to 0.21875
- forward_ids: int32 [4, 1024, 4], P('pipe', 'expert'), may hold values from 0 to 7, all different within a row; in each aligned block of 128 rows (0 to 127, 128 to 255, ..., all dimensions but the last counted through in order) at most 72 rows name the same one
- backward_input: bfloat16 [4, 1024, 2048], P('pipe', 'expert'), may hold values from -6 to 6
- backward_ids: int32 [4, 1024, 4], P('pipe', 'expert'), may hold values from 0 to 7, all different within a row; in each aligned block of 128 rows (0 to 127, 128 to 255, ..., all dimensions but the last counted through in order) at most 72 rows name the same one
- output_grad: bfloat16 [4, 1024, 2048], P('pipe', 'expert'), may hold values from -6 to 6
Outputs:
- forward_output: bfloat16 [4, 1024, 2048], P('pipe', 'expert')
- input_grad: bfloat16 [4, 1024, 2048], P('pipe', 'expert')
- router_grad: float32 [4, 2048, 8], P('pipe', 'expert')
- gain_grad: float32 [4, 2048], P('pipe', 'expert')
Inputs may be any that keep to these rules, and one draw needn't show every extreme that they name: `forward_ids`: each row names 4 different experts; in the 128 rows of one device no expert is named more than 72 times, and on some devices one is named exactly 72 times. `backward_ids`: each row names 4 different experts; in the 128 rows of one device no expert is named more than 72 times, and on some devices one is named exactly 72 times.
All inputs are finite; a program needn't handle non-finite values.
Results may differ from a plain program's by a relative error of at most 0.012.
Values may be sent and summed in bfloat16 or wider, within the bound.
A program may use at most 128 MiB of HBM per device.

v0:
```python
import jax
import jax.numpy as jnp
from jax import lax
from jax.experimental import pallas as pl
from jax.experimental.pallas import tpu as pltpu
from jax.sharding import PartitionSpec as P

HEADS = 16
KV_HEADS = 2
HEAD_DIM = 128


epsilon = 1e-06
far_below = -1e30


def extended(x, sides, width):
    for axis, dim in sides:
        devices, length = (lax.axis_size(axis), x.shape[dim])
        up = [(i, (i + 1) % devices) for i in range(devices)]
        down = [(j, i) for i, j in up]
        last = lax.slice_in_dim(x, length - width, length, axis=dim)
        leading = lax.slice_in_dim(x, 0, width, axis=dim)
        before = lax.ppermute(last, axis, up)
        after = lax.ppermute(leading, axis, down)
        x = jnp.concatenate([before, x, after], axis=dim)
    return x


def normalize(resid, gain):
    wide = resid.astype(jnp.float32)
    inv_rms = lax.rsqrt(jnp.mean(wide * wide, axis=-1, keepdims=True) + epsilon)
    return (wide, inv_rms, (wide * inv_rms * gain).astype(jnp.bfloat16))


def routing(normed, expert_ids, table):
    logits = jnp.dot(normed, table, preferred_element_type=jnp.float32)
    selects = expert_ids[:, :, None] == jnp.arange(table.shape[1], dtype=jnp.int32)
    chosen = jnp.sum(jnp.where(selects, logits[:, None, :], 0.0), axis=-1)
    route_probs = 1.0 / jnp.sum(jnp.exp(chosen[:, None, :] - chosen[:, :, None]), axis=-1)
    return (route_probs, selects)


def place_slots(selects, capacity):
    counted = selects.reshape(-1, selects.shape[-1]).astype(jnp.int32)
    running = jnp.cumsum(counted, axis=0)
    slot_index = jnp.sum(counted * running, axis=-1) - 1
    owner = jnp.sum(counted * jnp.arange(selects.shape[-1], dtype=jnp.int32), axis=-1)
    return (owner * capacity + slot_index).reshape(selects.shape[0], selects.shape[1])


def pack_rows(source_rows, target, experts, capacity):
    buffer = jnp.zeros((experts * capacity, source_rows.shape[1]), source_rows.dtype)
    spread = jnp.broadcast_to(source_rows[:, None, :], target.shape + (source_rows.shape[1],))
    return buffer.at[target].set(spread).reshape(experts, capacity, source_rows.shape[1])


def unpack_rows(buffer, target):
    return buffer.reshape((-1,) + buffer.shape[2:])[target]


def gather_slots(received, per_device):
    shaped = received.reshape((-1, per_device) + received.shape[1:])
    return jnp.swapaxes(shaped, 0, 1).reshape((per_device, -1) + received.shape[2:])


def scatter_slots(result, sources):
    shaped = result.reshape((result.shape[0], sources, -1) + result.shape[2:])
    return jnp.swapaxes(shaped, 0, 1).reshape((-1,) + shaped.shape[2:])


def attention(queries, new_keys, new_values, cache_keys, cache_values, length):
    tokens = queries.shape[0]
    context = cache_keys.shape[0]
    key_rows = jnp.concatenate([cache_keys, new_keys], axis=0).reshape(-1, KV_HEADS, HEAD_DIM)
    value_rows = jnp.concatenate([cache_values, new_values], axis=0).reshape(-1, KV_HEADS, HEAD_DIM)
    grouped = queries.reshape(tokens, KV_HEADS, HEADS // KV_HEADS, HEAD_DIM)
    scores = jnp.einsum(
        "tkgd,skd->kgts", grouped, key_rows, preferred_element_type=jnp.float32
    ) * HEAD_DIM ** (-0.5)
    position = jnp.arange(key_rows.shape[0], dtype=jnp.int32)[None, :]
    query_pos = jnp.arange(tokens, dtype=jnp.int32)[:, None]
    visible = jnp.where(position < context, position < length, position - context <= query_pos)
    scores = jnp.where(visible, scores, far_below)
    row_max = jnp.max(scores, axis=-1, keepdims=True)
    lifted = jnp.exp(scores - row_max)
    attn_weights = (lifted / jnp.sum(lifted, axis=-1, keepdims=True)).astype(jnp.bfloat16)
    merged = jnp.einsum(
        "kgts,skd->tkgd", attn_weights, value_rows, preferred_element_type=jnp.float32
    )
    return merged.reshape(tokens, HEADS * HEAD_DIM).astype(jnp.bfloat16)


def expert_ahead(slot_rows, gate_matrix, up_matrix, down_matrix):
    gate_pre = jnp.einsum(
        "erd,edf->erf", slot_rows, gate_matrix, preferred_element_type=jnp.float32
    )
    up_pre = jnp.einsum("erd,edf->erf", slot_rows, up_matrix, preferred_element_type=jnp.float32)
    hidden = (gate_pre * jax.nn.sigmoid(gate_pre) * up_pre).astype(jnp.bfloat16)
    return jnp.einsum(
        "erf,efd->erd", hidden, down_matrix, preferred_element_type=jnp.float32
    ).astype(jnp.bfloat16)


def expert_behind(slot_rows, slot_grads, gate_matrix, up_matrix, down_matrix):
    gate_pre = jnp.einsum(
        "erd,edf->erf", slot_rows, gate_matrix, preferred_element_type=jnp.float32
    )
    up_pre = jnp.einsum("erd,edf->erf", slot_rows, up_matrix, preferred_element_type=jnp.float32)
    sigmoid_gate = jax.nn.sigmoid(gate_pre)
    gate_act = gate_pre * sigmoid_gate
    hidden = (gate_act * up_pre).astype(jnp.bfloat16)
    down_grad = jnp.einsum(
        "erd,efd->erf", slot_grads, down_matrix, preferred_element_type=jnp.float32
    )
    weight_grad = jnp.sum(hidden.astype(jnp.float32) * down_grad, axis=-1).astype(jnp.bfloat16)
    slope_act = sigmoid_gate * (1.0 + gate_pre * (1.0 - sigmoid_gate))
    gate_grad = (down_grad * up_pre * slope_act).astype(jnp.bfloat16)
    up_grad = (down_grad * gate_act).astype(jnp.bfloat16)
    slot_back = jnp.einsum(
        "erf,edf->erd", gate_grad, gate_matrix, preferred_element_type=jnp.float32
    )
    slot_back = slot_back + jnp.einsum(
        "erf,edf->erd", up_grad, up_matrix, preferred_element_type=jnp.float32
    )
    return (slot_back.astype(jnp.bfloat16), weight_grad)


def routed_body(
    forward_input,
    queries,
    new_keys,
    new_values,
    cache_keys,
    cache_values,
    context_lengths,
    norm_gain,
    router,
    gate_weight,
    up_weight,
    down_weight,
    forward_ids,
    backward_input,
    backward_ids,
    output_grad,
):
    tokens = forward_input.shape[1]
    experts = router.shape[2]
    fan_out = forward_ids.shape[2]
    per_device = gate_weight.shape[1]
    sources = lax.axis_size("expert")
    capacity = max(2, tokens * fan_out // experts + max(1, tokens * fan_out // (8 * experts)))
    gain = norm_gain[0]
    table = router[0]
    gate_local = gate_weight[0]
    up_local = up_weight[0]
    down_local = down_weight[0]
    mixed = attention(
        queries[0],
        new_keys[0],
        new_values[0],
        cache_keys[0],
        cache_values[0],
        context_lengths[0, 0],
    )
    resid_ahead = (forward_input[0].astype(jnp.float32) + mixed.astype(jnp.float32)).astype(
        jnp.bfloat16
    )
    ahead_wide, ahead_inv, ahead_normed = normalize(resid_ahead, gain)
    ahead_probs, ahead_selects = routing(ahead_normed, forward_ids[0], table)
    ahead_target = place_slots(ahead_selects, capacity)
    ahead_buffer = pack_rows(ahead_normed, ahead_target, experts, capacity)
    behind_wide, behind_inv, behind_normed = normalize(backward_input[0], gain)
    behind_probs, behind_selects = routing(behind_normed, backward_ids[0], table)
    behind_target = place_slots(behind_selects, capacity)
    rows_buffer = pack_rows(behind_normed, behind_target, experts, capacity)
    grads_buffer = pack_rows(output_grad[0], behind_target, experts, capacity)
    arrived = lax.all_to_all(ahead_buffer, "expert", split_axis=0, concat_axis=0, tiled=True)
    produced = scatter_slots(
        expert_ahead(gather_slots(arrived, per_device), gate_local, up_local, down_local), sources
    )
    returned, behind_rows, behind_grads = (
        lax.all_to_all(produced, "expert", split_axis=0, concat_axis=0, tiled=True),
        lax.all_to_all(rows_buffer, "expert", split_axis=0, concat_axis=0, tiled=True),
        lax.all_to_all(grads_buffer, "expert", split_axis=0, concat_axis=0, tiled=True),
    )
    slot_back, slot_weight = expert_behind(
        gather_slots(behind_rows, per_device),
        gather_slots(behind_grads, per_device),
        gate_local,
        up_local,
        down_local,
    )
    input_back, weight_back = (
        lax.all_to_all(
            scatter_slots(slot_back, sources), "expert", split_axis=0, concat_axis=0, tiled=True
        ),
        lax.all_to_all(
            scatter_slots(slot_weight, sources), "expert", split_axis=0, concat_axis=0, tiled=True
        ),
    )
    ahead_rows = unpack_rows(returned, ahead_target).astype(jnp.float32)
    ahead_output = (ahead_wide + jnp.sum(ahead_probs[:, :, None] * ahead_rows, axis=1)).astype(
        jnp.bfloat16
    )
    input_rows = unpack_rows(input_back, behind_target).astype(jnp.float32)
    weight_rows = weight_back.reshape(-1)[behind_target].astype(jnp.float32)
    normed_grad = jnp.sum(behind_probs[:, :, None] * input_rows, axis=1)
    logit_terms = behind_probs * (
        weight_rows - jnp.sum(behind_probs * weight_rows, axis=-1, keepdims=True)
    )
    logit_grad = jnp.sum(jnp.where(behind_selects, logit_terms[:, :, None], 0.0), axis=1).astype(
        jnp.bfloat16
    )
    normed_grad = normed_grad + jnp.dot(logit_grad, table.T, preferred_element_type=jnp.float32)
    grad_factor = (tokens * sources) ** (-0.5)
    router_term = (
        jnp.dot(behind_normed.T, logit_grad, preferred_element_type=jnp.float32) * grad_factor
    )
    scaled_grad = normed_grad * gain
    resid_grad = behind_inv * (
        scaled_grad
        - behind_wide
        * behind_inv
        * behind_inv
        * jnp.mean(scaled_grad * behind_wide, axis=-1, keepdims=True)
    )
    gain_term = jnp.sum(normed_grad * behind_wide * behind_inv, axis=0) * grad_factor
    input_grad = (output_grad[0].astype(jnp.float32) + resid_grad).astype(jnp.bfloat16)
    router_part, gain_part = (
        lax.psum_scatter(router_term, "expert", scatter_dimension=0, tiled=True),
        lax.psum_scatter(gain_term, "expert", scatter_dimension=0, tiled=True),
    )
    crossing = extended(jnp.stack([input_grad, ahead_output]), (("pipe", 0),), 1)
    return (crossing[0][None], crossing[3][None], router_part[None], gain_part[None])


TILE = 256
SUB = 2
VMEM_LIMIT = 60 * 2**20


def fits(operands):
    experts, fan_out = (operands[8].shape[2], operands[12].shape[2])
    tokens, width = operands[0].shape[1:]
    hidden = operands[9].shape[3]
    return (
        lax.axis_size("expert") == 2**3
        and experts == lax.axis_size("expert")
        and experts <= 2 * fan_out
        and lax.axis_size("pipe") > 1
        and tokens == HEAD_DIM
        and operands[4].shape[1] == tokens
        and width % TILE == 0
        and hidden % TILE == 0
    )


def section_kernel(
    length_ref,
    fin_ref,
    q_ref,
    nk_ref,
    nv_ref,
    ck_ref,
    cv_ref,
    gain_ref,
    router_ref,
    gate_ref,
    up_ref,
    down_ref,
    fids_ref,
    bin_ref,
    bids_ref,
    og_ref,
    out_fwd,
    out_back,
    out_sums,
    gat,
    gate_v,
    up_v,
    down_v,
    part,
    sibr,
    rx,
    act_a,
    act_b,
    wacc,
    pcol,
    ptab,
    wgs,
    wgr,
    rgp,
    rgr,
    x_v,
    fin_v,
    q_v,
    k_v,
    v_v,
    resid_v,
    staged,
    table,
    lg_rows,
    gacc,
    local_sem,
    gsend,
    grecv,
    ssend,
    srecv,
    xsend,
    xrecv,
    zsend,
    zrecv,
    tsend,
    trecv,
):
    tokens, width = fin_ref.shape
    hidden_tiles = gate_v.shape[0]
    wide_tiles = width // TILE
    half = tokens // 2
    small = half // SUB
    experts = ptab.shape[2]
    group = ptab.shape[1]
    heads = width // HEAD_DIM
    f32, bf16 = jnp.float32, jnp.bfloat16
    nt = (((1,), (1,)), ((), ()))

    me = lax.axis_index("expert")
    core, at_x, at_y = me % 2, (me // 2) % 2, me // 4
    pipe, pipes = lax.axis_index("pipe"), lax.axis_size("pipe")
    following, previous = (pipe + 1) % pipes, (pipe + pipes - 1) % pipes

    def peer(j):
        a = 1 - core if j % 2 else core
        b = 1 - at_x if (j // 2) % 2 else at_x
        c = 1 - at_y if j // 4 else at_y
        return (c * 2 + b) * 2 + a

    def at(j):
        return {"expert": peer(j)}

    SIB, XN, YN = 1, 2, 4

    def remote(src, dst, send, recv, where):
        return pltpu.make_async_remote_copy(
            src_ref=src,
            dst_ref=dst,
            send_sem=send,
            recv_sem=recv,
            device_id=where,
            device_id_type=pl.DeviceIdType.MESH,
        )

    gather_plan = (
        (0, 0, 0, tokens, tokens, SIB),
        (0, 0, 1, 0, half, XN),
        (0, half, 1, half, half, XN),
        (0, half, 2, half, half, YN),
        (0, 0, 2, 0, half, YN),
        (1, 0, 3, 0, half, YN),
        (2, half, 3, half, half, XN),
        (1, 0, 1, tokens, half, SIB),
        (1, half, 1, tokens + half, half, SIB),
        (2, 0, 2, tokens, half, SIB),
        (2, half, 2, tokens + half, half, SIB),
        (3, 0, 3, tokens, half, SIB),
        (3, half, 3, tokens + half, half, SIB),
    )

    def gcopy(a, i):
        sb, sr, tb, tr, rows, j = gather_plan[i]
        return remote(
            gat.at[a, sb, pl.ds(sr, rows)],
            gat.at[a, tb, pl.ds(tr, rows)],
            gsend.at[a, i],
            grecv.at[a, i],
            at(j),
        )

    def scopy(m, r):
        return remote(
            part.at[m, r, pl.ds(tokens, tokens)],
            sibr.at[m, r],
            ssend.at[m, r],
            srecv.at[m, r],
            at(SIB),
        )

    reduce_plan = ((3, 0, XN), (1, 0, XN), (1, half, XN), (3, half, YN), (2, half, YN), (2, 0, YN))

    def xcopy(m, k, q):
        r, row, j = reduce_plan[k]
        return remote(
            part.at[m, r, pl.ds(row + q * small, small)],
            rx.at[m, k, pl.ds(q * small, small)],
            xsend.at[m, k, q],
            xrecv.at[m, k, q],
            at(j),
        )

    def zcopy(m, i):
        rows = pl.ds(i * small, small)
        out, there = (out_fwd, following) if m else (out_back, previous)
        return remote(
            staged.at[m, rows], out.at[rows], zsend.at[m, i], zrecv.at[m, i], {"pipe": there}
        )

    def tcopy(kind, j):
        src, dst = (
            (ptab.at[0, 0], ptab.at[0, j]),
            (ptab.at[1, 0], ptab.at[1, j]),
            (wgs.at[j], wgr.at[j]),
            (rgp.at[peer(j)], rgr.at[j]),
        )[kind]
        return remote(src, dst, tsend.at[kind, j], trecv.at[kind, j], at(j))

    loads = [
        (og_ref, gat.at[0, 0, pl.ds(0, tokens)]),
        (bin_ref, x_v),
        (q_ref, q_v),
        (ck_ref, k_v.at[pl.ds(0, tokens)]),
        (nk_ref, k_v.at[pl.ds(tokens, tokens)]),
        (cv_ref, v_v.at[pl.ds(0, tokens)]),
        (nv_ref, v_v.at[pl.ds(tokens, tokens)]),
        (fin_ref, fin_v),
    ]
    for t in range(hidden_tiles):
        cols = pl.ds(t * TILE, TILE)
        loads += [
            (gate_ref.at[:, cols], gate_v.at[t]),
            (up_ref.at[:, cols], up_v.at[t]),
            (down_ref.at[cols], down_v.at[t]),
        ]
    loads = [
        pltpu.make_async_copy(src, dst, local_sem.at[i]) for i, (src, dst) in enumerate(loads)
    ]
    for copy in loads:
        copy.start()

    barrier = pltpu.get_barrier_semaphore()
    for j in range(1, group):
        pl.semaphore_signal(barrier, inc=1, device_id=at(j), device_id_type=pl.DeviceIdType.MESH)
    for there in (following, previous):
        pl.semaphore_signal(
            barrier, inc=1, device_id={"pipe": there}, device_id_type=pl.DeviceIdType.MESH
        )
    pl.semaphore_wait(barrier, group - 1 + 2)

    loads[0].wait()
    for i in (1, 3, 2, 4, 0):
        gcopy(0, i).start()

    table[...] = jnp.zeros_like(table)
    table[0 : router_ref.shape[0], :] = router_ref[...]
    gain = gain_ref[...]

    def normalize_rows(source, a):
        def step(i, carry):
            rows = pl.ds(pl.multiple_of(i * 32, 32), 32)
            x = source[rows, :].astype(f32)
            inv = lax.rsqrt(jnp.mean(x * x, axis=-1, keepdims=True) + epsilon)
            gat[a, 0, rows, :] = (x * inv * gain_ref[...]).astype(bf16)
            return carry

        lax.fori_loop(0, tokens // 32, step, 0)

    expert_row = lax.broadcasted_iota(jnp.int32, (experts, tokens), 0)

    def chosen_mask(ids_ref):
        ids = ids_ref[...]
        mask = ids[0:1, :] == expert_row
        for k in range(1, ids.shape[0]):
            mask = mask | (ids[k : k + 1, :] == expert_row)
        return mask

    def route(a, ids_ref, m):
        logits = lax.dot_general(
            table[...], gat[a, 0, 0:tokens, :], nt, preferred_element_type=f32
        )[0:experts, :]
        mask = chosen_mask(ids_ref)
        top = jnp.max(jnp.where(mask, logits, far_below), axis=0, keepdims=True)
        lifted = jnp.where(mask, jnp.exp(jnp.where(mask, logits - top, 0.0)), 0.0)
        ptab[m, 0] = lifted / jnp.sum(lifted, axis=0, keepdims=True)

    loads[1].wait()
    normalize_rows(x_v, 1)
    for i in (1, 3, 2, 4, 0):
        gcopy(1, i).start()
    route(1, bids_ref, 0)
    for j in range(1, group):
        tcopy(0, j).start()

    for i in range(2, 8):
        loads[i].wait()
    length = length_ref[0, 0]

    def one_head(h, carry):
        cols = pl.ds(pl.multiple_of(h * HEAD_DIM, HEAD_DIM), HEAD_DIM)
        shared = h // (HEADS // KV_HEADS)
        kv_cols = pl.ds(pl.multiple_of(shared * HEAD_DIM, HEAD_DIM), HEAD_DIM)
        scores = lax.dot_general(
            q_v[:, cols], k_v[:, kv_cols], nt, preferred_element_type=f32
        ) * HEAD_DIM ** (-0.5)
        position = lax.broadcasted_iota(jnp.int32, scores.shape, 1)
        query_pos = lax.broadcasted_iota(jnp.int32, scores.shape, 0)
        visible = ((position < tokens) & (position < length)) | (
            (position >= tokens) & (position - tokens <= query_pos)
        )
        scores = jnp.where(visible, scores, far_below)
        lifted = jnp.exp(scores - jnp.max(scores, axis=-1, keepdims=True))
        weights = (lifted / jnp.sum(lifted, axis=-1, keepdims=True)).astype(bf16)
        mixed = jnp.dot(weights, v_v[:, kv_cols], preferred_element_type=f32).astype(bf16)
        resid_v[:, cols] = (fin_v[:, cols].astype(f32) + mixed.astype(f32)).astype(bf16)
        return carry

    lax.fori_loop(0, heads, one_head, 0)
    normalize_rows(resid_v, 2)
    route(2, fids_ref, 1)
    for j in range(1, group):
        tcopy(1, j).start()
    for copy in loads[8:]:
        copy.wait()
    for kind in (0, 1):
        for j in range(1, group):
            tcopy(kind, j).wait_recv()

    def share_column(m, r):
        for s in range(2):
            row = jnp.sum(jnp.where(expert_row == me, ptab[m, 2 * r + s], 0.0), axis=0, keepdims=True)
            pcol[s * tokens : (s + 1) * tokens, :] = jnp.broadcast_to(row, (tokens, tokens)).T

    def behind_block(r):
        wacc[...] = jnp.zeros_like(wacc)

        def tile(t, carry):
            rows = gat[1, r]
            gate_pre = jnp.dot(rows, gate_v[t], preferred_element_type=f32)
            up_pre = jnp.dot(rows, up_v[t], preferred_element_type=f32)
            down_grad = lax.dot_general(gat[0, r], down_v[t], nt, preferred_element_type=f32)
            sig = jax.nn.sigmoid(gate_pre)
            gate_act = gate_pre * sig
            weighed = (gate_act * up_pre).astype(bf16).astype(f32) * down_grad
            folded = weighed[:, 0:tokens]
            for c in range(1, TILE // tokens):
                folded = folded + weighed[:, c * tokens : (c + 1) * tokens]
            wacc[...] += folded
            slope = sig * (1.0 + gate_pre * (1.0 - sig))
            act_a[t] = (down_grad * up_pre * slope).astype(bf16)
            act_b[t] = (down_grad * gate_act).astype(bf16)
            return carry

        lax.fori_loop(0, hidden_tiles, tile, 0)
        for s in range(2):
            row = jnp.sum(wacc[s * tokens : (s + 1) * tokens, :].T, axis=0, keepdims=True)
            wgs[2 * r + s] = jnp.where(expert_row == me, row, 0.0)
        share_column(0, r)

        def back(n, carry):
            cols = pl.ds(pl.multiple_of(n * TILE, TILE), TILE)
            total = jnp.zeros((2 * tokens, TILE), f32)
            for t in range(hidden_tiles):
                total += lax.dot_general(act_a[t], gate_v[t, cols, :], nt, preferred_element_type=f32)
                total += lax.dot_general(act_b[t], up_v[t, cols, :], nt, preferred_element_type=f32)
            part[0, r, :, cols] = (total * pcol[:, 0:1]).astype(bf16)
            return carry

        lax.fori_loop(0, wide_tiles, back, 0)

    def ahead_block(r):
        def tile(t, carry):
            rows = gat[2, r]
            gate_pre = jnp.dot(rows, gate_v[t], preferred_element_type=f32)
            up_pre = jnp.dot(rows, up_v[t], preferred_element_type=f32)
            act_a[t] = (gate_pre * jax.nn.sigmoid(gate_pre) * up_pre).astype(bf16)
            return carry

        lax.fori_loop(0, hidden_tiles, tile, 0)
        share_column(1, r)

        def out(n, carry):
            cols = pl.ds(pl.multiple_of(n * TILE, TILE), TILE)
            total = jnp.zeros((2 * tokens, TILE), f32)
            for t in range(hidden_tiles):
                total += jnp.dot(act_a[t], down_v[t, :, cols], preferred_element_type=f32)
            part[1, r, :, cols] = (total * pcol[:, 0:1]).astype(bf16)
            return carry

        lax.fori_loop(0, wide_tiles, out, 0)

    def add_rows(m, r, base, count, other, other_base):
        def step(i, carry):
            to = pl.ds(pl.multiple_of(base + i * 32, 32), 32)
            since = pl.ds(pl.multiple_of(other_base + i * 32, 32), 32)
            part[m, r, to, :] = (
                part[m, r, to, :].astype(f32) + other[since, :].astype(f32)
            ).astype(bf16)
            return carry

        lax.fori_loop(0, count // 32, step, 0)

    def join_sibling(m, r):
        scopy(m, r).wait_recv()
        add_rows(m, r, 0, tokens, sibr.at[m, r], 0)

    def first_phase(m):
        join_sibling(m, 3)
        for q in range(SUB):
            xcopy(m, 0, q).start()
            xcopy(m, 3, q).start()
        join_sibling(m, 1)
        for q in range(SUB):
            xcopy(m, 1, q).start()
        join_sibling(m, 2)
        for q in range(SUB):
            xcopy(m, 4, q).start()
        join_sibling(m, 0)

    def second_phase(m):
        for q in range(SUB):
            xcopy(m, 0, q).wait_recv()
            add_rows(m, 2, q * small, small, rx.at[m, 0], q * small)
            xcopy(m, 5, q).start()
            xcopy(m, 3, q).wait_recv()
            add_rows(m, 1, half + q * small, small, rx.at[m, 3], q * small)
            xcopy(m, 2, q).start()

    def forward_first(a):
        gcopy(a, 1).wait_recv()
        gcopy(a, 5).start()
        gcopy(a, 7).start()
        gcopy(a, 3).wait_recv()
        gcopy(a, 6).start()
        gcopy(a, 10).start()

    def forward_second(a):
        gcopy(a, 2).wait_recv()
        gcopy(a, 8).start()
        gcopy(a, 4).wait_recv()
        gcopy(a, 9).start()

    def forward_third(a):
        gcopy(a, 5).wait_recv()
        gcopy(a, 11).start()
        gcopy(a, 6).wait_recv()
        gcopy(a, 12).start()

    def arrived(a, *which):
        for i in which:
            gcopy(a, i).wait_recv()

    forward_first(0)

    def stage(step, carry):
        @pl.when(step == 0)
        def _():
            arrived(0, 0)
            arrived(1, 0)

        @pl.when(step == 1)
        def _():
            forward_second(0)
            forward_first(1)
            forward_second(1)
            for i in (1, 3, 2, 4, 0):
                gcopy(2, i).start()
            arrived(0, 7, 8)
            arrived(1, 7, 8)

        @pl.when(step == 2)
        def _():
            arrived(0, 9, 10)
            arrived(1, 9, 10)

        @pl.when(step == 3)
        def _():
            forward_third(0)
            forward_third(1)
            arrived(0, 11, 12)
            arrived(1, 11, 12)

        @pl.when(step == 4)
        def _():
            for j in range(1, group):
                tcopy(2, j).start()
            forward_first(2)
            first_phase(0)
            arrived(2, 0)

        @pl.when(step == 5)
        def _():
            forward_second(2)
            arrived(2, 7, 8)

        @pl.when(step == 6)
        def _():
            arrived(2, 9, 10)

        @pl.when(step == 7)
        def _():
            second_phase(0)
            forward_third(2)
            arrived(2, 11, 12)

        @pl.when(step < 4)
        def _():
            behind_block(step)

        @pl.when(step >= 4)
        def _():
            ahead_block(step - 4)

        for s in range(8):

            @pl.when(step == s)
            def _(s=s):
                scopy(s // 4, s % 4).start()

        return carry

    lax.fori_loop(0, 8, stage, 0)
    first_phase(1)

    wrows = wgs[0]
    for j in range(1, group):
        tcopy(2, j).wait_recv()
        wrows = wrows + wgr[j]
    probs = ptab[0, 0]
    logit_grad = probs * (wrows - jnp.sum(probs * wrows, axis=0, keepdims=True))
    padded = jnp.concatenate([logit_grad, jnp.zeros((tokens - experts, tokens), f32)], axis=0)
    lg_rows[...] = padded.T.astype(bf16)
    gacc[...] = jnp.zeros_like(gacc)

    def total_rows(m, i):
        rows = pl.ds(i * small, small)
        side, q = i // SUB, i % SUB
        inner = pl.ds(q * small, small)
        near, far = (4, 2) if side else (1, 5)
        xcopy(m, near, q).wait_recv()
        xcopy(m, far, q).wait_recv()
        return rows, near, far, inner

    def finish_behind(i):
        rows, near, far, inner = total_rows(0, i)
        for u in range(small // 16):
            at_rows = pl.ds(i * small + u * 16, 16)
            sub_rows = pl.ds((i % SUB) * small + u * 16, 16)
            normed_grad = (
                part[0, 0, at_rows, :].astype(f32)
                + rx[0, near, sub_rows, :].astype(f32)
                + rx[0, far, sub_rows, :].astype(f32)
                + jnp.dot(lg_rows[at_rows, :], table[...], preferred_element_type=f32)
            )
            x = x_v[at_rows, :].astype(f32)
            inv = lax.rsqrt(jnp.mean(x * x, axis=-1, keepdims=True) + epsilon)
            scaled = normed_grad * gain_ref[...]
            slope = jnp.mean(scaled * x, axis=-1, keepdims=True)
            resid_grad = inv * (scaled - x * (inv * inv * slope))
            gacc[...] += jnp.sum(normed_grad * x * inv, axis=0, keepdims=True)
            staged[0, at_rows, :] = (
                gat[0, 0, at_rows, :].astype(f32) + resid_grad
            ).astype(bf16)
        zcopy(0, i).start()

    def finish_ahead(i):
        rows, near, far, inner = total_rows(1, i)
        total = (
            part[1, 0, rows, :].astype(f32)
            + rx[1, near, inner, :].astype(f32)
            + rx[1, far, inner, :].astype(f32)
        )
        staged[1, rows, :] = (resid_v[rows, :].astype(f32) + total).astype(bf16)
        zcopy(1, i).start()

    order = [side * SUB + q for q in range(SUB) for side in range(2)]
    for i in order:
        finish_behind(i)

    second_phase(1)
    factor = (tokens * group) ** (-0.5)
    pad_rows = rgp.shape[1]
    lg_short = padded[0:pad_rows, :].astype(bf16)
    span = rgp.shape[2]
    which = lax.broadcasted_iota(jnp.int32, (pad_rows, span), 0)
    for d in range(group):
        cols = slice(d * span, (d + 1) * span)
        grads = jnp.dot(lg_short, gat[1, 0, 0:tokens, cols], preferred_element_type=f32)
        rgp[d] = jnp.where(which == experts, gacc[:, cols], grads) * factor
    for j in range(1, group):
        tcopy(3, j).start()

    for i in order:
        finish_ahead(i)

    sums = rgp[me]
    for j in range(1, group):
        tcopy(3, j).wait_recv()
        sums = sums + rgr[j]
    out_sums[...] = sums

    for a in range(3):
        for i in range(len(gather_plan)):
            gcopy(a, i).wait_send()
    for kind in range(4):
        for j in range(1, group):
            tcopy(kind, j).wait_send()
    for m in range(2):
        for r in range(4):
            scopy(m, r).wait_send()
        for k in range(len(reduce_plan)):
            for q in range(SUB):
                xcopy(m, k, q).wait_send()
        for i in range(2 * SUB):
            zcopy(m, i).wait()


def kernel_body(
    forward_input,
    queries,
    new_keys,
    new_values,
    cache_keys,
    cache_values,
    context_lengths,
    norm_gain,
    router,
    gate_weight,
    up_weight,
    down_weight,
    forward_ids,
    backward_input,
    backward_ids,
    output_grad,
):
    tokens, width = forward_input.shape[1:]
    experts = router.shape[2]
    group = lax.axis_size("expert")
    hidden = gate_weight.shape[3]
    tiles = hidden // TILE
    pad_experts = experts + 8
    half = tokens // 2
    kv_width = cache_keys.shape[2]
    f32, bf16 = jnp.float32, jnp.bfloat16
    table = jnp.pad(router[0].T, ((0, pad_experts - experts), (0, 0)))
    hbm = pl.BlockSpec(memory_space=pl.ANY)
    near = pl.BlockSpec(memory_space=pltpu.VMEM)
    copies = 13
    dma = pltpu.SemaphoreType.DMA
    out_fwd, out_back, sums = pl.pallas_call(
        section_kernel,
        out_shape=(
            jax.ShapeDtypeStruct((tokens, width), bf16),
            jax.ShapeDtypeStruct((tokens, width), bf16),
            jax.ShapeDtypeStruct((pad_experts, width // group), f32),
        ),
        in_specs=[
            pl.BlockSpec(memory_space=pltpu.SMEM),
            hbm,
            hbm,
            hbm,
            hbm,
            hbm,
            hbm,
            near,
            near,
            hbm,
            hbm,
            hbm,
            near,
            hbm,
            near,
            hbm,
        ],
        out_specs=(hbm, hbm, near),
        scratch_shapes=[
            pltpu.VMEM((3, 4, 2 * tokens, width), bf16),
            pltpu.VMEM((tiles, width, TILE), bf16),
            pltpu.VMEM((tiles, width, TILE), bf16),
            pltpu.VMEM((tiles, TILE, width), bf16),
            pltpu.VMEM((2, 4, 2 * tokens, width), bf16),
            pltpu.VMEM((2, 4, tokens, width), bf16),
            pltpu.VMEM((2, 6, half, width), bf16),
            pltpu.VMEM((tiles, 2 * tokens, TILE), bf16),
            pltpu.VMEM((tiles, 2 * tokens, TILE), bf16),
            pltpu.VMEM((2 * tokens, tokens), f32),
            pltpu.VMEM((2 * tokens, tokens), f32),
            pltpu.VMEM((2, group, experts, tokens), f32),
            pltpu.VMEM((group, experts, tokens), f32),
            pltpu.VMEM((group, experts, tokens), f32),
            pltpu.VMEM((group, pad_experts, width // group), f32),
            pltpu.VMEM((group, pad_experts, width // group), f32),
            pltpu.VMEM((tokens, width), bf16),
            pltpu.VMEM((tokens, width), bf16),
            pltpu.VMEM((tokens, width), bf16),
            pltpu.VMEM((2 * tokens, kv_width), bf16),
            pltpu.VMEM((2 * tokens, kv_width), bf16),
            pltpu.VMEM((tokens, width), bf16),
            pltpu.VMEM((2, tokens, width), bf16),
            pltpu.VMEM((tokens, width), bf16),
            pltpu.VMEM((tokens, tokens), bf16),
            pltpu.VMEM((1, width), f32),
            dma((8 + 3 * tiles,)),
            dma((3, copies)),
            dma((3, copies)),
            dma((2, 4)),
            dma((2, 4)),
            dma((2, 6, SUB)),
            dma((2, 6, SUB)),
            dma((2, 2 * SUB)),
            dma((2, 2 * SUB)),
            dma((4, group)),
            dma((4, group)),
        ],
        compiler_params=pltpu.CompilerParams(
            collective_id=0, has_side_effects=True, vmem_limit_bytes=VMEM_LIMIT
        ),
    )(
        context_lengths,
        forward_input[0],
        queries[0],
        new_keys[0],
        new_values[0],
        cache_keys[0],
        cache_values[0],
        norm_gain,
        table,
        gate_weight[0, 0],
        up_weight[0, 0],
        down_weight[0, 0],
        forward_ids[0].T,
        backward_input[0],
        backward_ids[0].T,
        output_grad[0],
    )
    return (out_fwd[None], out_back[None], sums[:experts].T[None], sums[experts][None])


def body(*operands):
    return (kernel_body if fits(operands) else routed_body)(*operands)


def solution(mesh):
    placed = (
        P("pipe", "expert", None),
        P("pipe", "expert", None),
        P("pipe", "expert", None),
        P("pipe", "expert", None),
        P("pipe", "expert", None),
        P("pipe", "expert", None),
        P("pipe", "expert"),
        P("pipe", None),
        P("pipe", None, None),
        P("pipe", "expert", None, None),
        P("pipe", "expert", None, None),
        P("pipe", "expert", None, None),
        P("pipe", "expert", None),
        P("pipe", "expert", None),
        P("pipe", "expert", None),
        P("pipe", "expert", None),
    )
    return jax.shard_map(
        body,
        mesh=mesh,
        in_specs=placed,
        out_specs=(
            P("pipe", "expert", None),
            P("pipe", "expert", None),
            P("pipe", "expert", None),
            P("pipe", "expert"),
        ),
        check_vma=False,
    )
```

profile of v0, /device:TPU:0, one launch (start us, length us, event | category | flops | bytes accessed | tf_op | source)
XLA Modules:
  0.0 132.4 jit_solution(11043047986549558759)
XLA Ops:
  0.6 1.4 %pad.4.router_ref = bf16[16,2048]{1,0:T(8,128)(2,1)} pad(bf16[8,2048]{1,0:T(8,128)(2,1)} %bitcast.39, bf16[]{:T(256)} %constant.2.clone.1), padding=0_8x0_0 | pad | bytes 98306 | tf_op jit(solution)/shard_map/jit(_pad)/pad | solution.py:843
  2.7 123.4 %shard_map.183 = (bf16[128,2048]{1,0:T(8,128)(2,1)}, bf16[128,2048]{1,0:T(8,128)(2,1)}, f32[16,256]{1,0:T(8,128)}) custom-call(s32[1,1]{1,0:T(1,128)S(6)} %copy.22.length_ref, bf16[128,2048]{1,0:T(8,128)(2,1)} %bitcast.29, bf16[128,2048]{1,0:T(8,128)(2,1)} %bitcast.30, bf16[128,256]{1,0:T(8,128)(2,1)} %bitcast.35, bf16[128,256]{1,0:T(8,128)(2,1)} %bitcast.36, ...), custom_call_target="tpu_custom_call" | custom-call | tf_op jit(solution)/shard_map/pallas_call | solution.py:848
  126.0 1.3 slice_bitcast_fusion
  127.3 1.3 slice.7
  128.6 1.9 %copy.23 = bf16[1,128,2048]{2,1,0:T(8,128)(2,1)} copy(bf16[1,128,2048]{2,1,0:T(8,128)(2,1)} %bitcast.34) | data formatting | bytes 1048576
  130.5 1.9 %copy.24 = bf16[1,128,2048]{2,1,0:T(8,128)(2,1)} copy(bf16[1,128,2048]{2,1,0:T(8,128)(2,1)} %bitcast.33) | data formatting | bytes 1048576
where the time goes:
time: 133 us; the launch traced here: 132 us
  Pallas kernels  123 us (92%)
  local copies, waits for them, and re-layouts  7.71 us (6%)
    pallas_call x1, Pallas kernels, kernel_body(): pl.pallas_call(section_kernel, out_shape=(jax.ShapeDtypeStruct((tokens, w...  123 us
    unnamed x2, local copies, waits for them, and re-layouts  3.76 us

commit v1 on v0

--- a/solution.py
+++ b/solution.py
@@ -236,7 +236,8 @@
 
 
 TILE = 256
-SUB = 2
+SUB = 4
+AT_ONCE = 2
 VMEM_LIMIT = 60 * 2**20
 
 
@@ -451,8 +452,10 @@
         gcopy(0, i).start()
 
     table[...] = jnp.zeros_like(table)
-    table[0 : router_ref.shape[0], :] = router_ref[...]
-    gain = gain_ref[...]
+    rows16 = rgp.shape[1]
+    table[0:rows16, :] = jnp.concatenate(
+        [router_ref[...].astype(f32), jnp.zeros((rows16 - experts, width), f32)], axis=0
+    ).astype(bf16)
 
     def normalize_rows(source, a):
         def step(i, carry):
@@ -494,26 +497,33 @@
         loads[i].wait()
     length = length_ref[0, 0]
 
-    def one_head(h, carry):
-        cols = pl.ds(pl.multiple_of(h * HEAD_DIM, HEAD_DIM), HEAD_DIM)
-        shared = h // (HEADS // KV_HEADS)
+    position = lax.broadcasted_iota(jnp.int32, (tokens, 2 * tokens), 1)
+    query_pos = lax.broadcasted_iota(jnp.int32, (tokens, 2 * tokens), 0)
+    visible = ((position < tokens) & (position < length)) | (
+        (position >= tokens) & (position - tokens <= query_pos)
+    )
+
+    def some_heads(i, carry):
+        shared = i // (HEADS // KV_HEADS // AT_ONCE)
         kv_cols = pl.ds(pl.multiple_of(shared * HEAD_DIM, HEAD_DIM), HEAD_DIM)
-        scores = lax.dot_general(
-            q_v[:, cols], k_v[:, kv_cols], nt, preferred_element_type=f32
-        ) * HEAD_DIM ** (-0.5)
-        position = lax.broadcasted_iota(jnp.int32, scores.shape, 1)
-        query_pos = lax.broadcasted_iota(jnp.int32, scores.shape, 0)
-        visible = ((position < tokens) & (position < length)) | (
-            (position >= tokens) & (position - tokens <= query_pos)
-        )
-        scores = jnp.where(visible, scores, far_below)
-        lifted = jnp.exp(scores - jnp.max(scores, axis=-1, keepdims=True))
-        weights = (lifted / jnp.sum(lifted, axis=-1, keepdims=True)).astype(bf16)
-        mixed = jnp.dot(weights, v_v[:, kv_cols], preferred_element_type=f32).astype(bf16)
-        resid_v[:, cols] = (fin_v[:, cols].astype(f32) + mixed.astype(f32)).astype(bf16)
+        keys, values = k_v[:, kv_cols], v_v[:, kv_cols]
+        results = []
+        for u in range(AT_ONCE):
+            h = i * AT_ONCE + u
+            cols = pl.ds(pl.multiple_of(h * HEAD_DIM, HEAD_DIM), HEAD_DIM)
+            scores = lax.dot_general(q_v[:, cols], keys, nt, preferred_element_type=f32)
+            scores = jnp.where(visible, scores * HEAD_DIM ** (-0.5), far_below)
+            lifted = jnp.exp(scores - jnp.max(scores, axis=-1, keepdims=True))
+            weights = (lifted / jnp.sum(lifted, axis=-1, keepdims=True)).astype(bf16)
+            mixed = jnp.dot(weights, values, preferred_element_type=f32).astype(bf16)
+            results.append(
+                (cols, (fin_v[:, cols].astype(f32) + mixed.astype(f32)).astype(bf16))
+            )
+        for cols, rows in results:
+            resid_v[:, cols] = rows
         return carry
 
-    lax.fori_loop(0, heads, one_head, 0)
+    lax.fori_loop(0, heads // AT_ONCE, some_heads, 0)
     normalize_rows(resid_v, 2)
     route(2, fids_ref, 1)
     for j in range(1, group):
@@ -589,31 +599,24 @@
 
     def add_rows(m, r, base, count, other, other_base):
         def step(i, carry):
-            to = pl.ds(pl.multiple_of(base + i * 32, 32), 32)
-            since = pl.ds(pl.multiple_of(other_base + i * 32, 32), 32)
+            to = pl.ds(pl.multiple_of(base + i * 16, 16), 16)
+            since = pl.ds(pl.multiple_of(other_base + i * 16, 16), 16)
             part[m, r, to, :] = (
                 part[m, r, to, :].astype(f32) + other[since, :].astype(f32)
             ).astype(bf16)
             return carry
 
-        lax.fori_loop(0, count // 32, step, 0)
+        lax.fori_loop(0, count // 16, step, 0)
 
     def join_sibling(m, r):
         scopy(m, r).wait_recv()
         add_rows(m, r, 0, tokens, sibr.at[m, r], 0)
 
-    def first_phase(m):
-        join_sibling(m, 3)
+    def send_block(m, r):
+        join_sibling(m, r)
         for q in range(SUB):
-            xcopy(m, 0, q).start()
-            xcopy(m, 3, q).start()
-        join_sibling(m, 1)
-        for q in range(SUB):
-            xcopy(m, 1, q).start()
-        join_sibling(m, 2)
-        for q in range(SUB):
-            xcopy(m, 4, q).start()
-        join_sibling(m, 0)
+            for k in ((), (1,), (4,), (0, 3))[r]:
+                xcopy(m, k, q).start()
 
     def second_phase(m):
         for q in range(SUB):
@@ -647,88 +650,6 @@
     def arrived(a, *which):
         for i in which:
             gcopy(a, i).wait_recv()
-
-    forward_first(0)
-
-    def stage(step, carry):
-        @pl.when(step == 0)
-        def _():
-            arrived(0, 0)
-            arrived(1, 0)
-
-        @pl.when(step == 1)
-        def _():
-            forward_second(0)
-            forward_first(1)
-            forward_second(1)
-            for i in (1, 3, 2, 4, 0):
-                gcopy(2, i).start()
-            arrived(0, 7, 8)
-            arrived(1, 7, 8)
-
-        @pl.when(step == 2)
-        def _():
-            arrived(0, 9, 10)
-            arrived(1, 9, 10)
-
-        @pl.when(step == 3)
-        def _():
-            forward_third(0)
-            forward_third(1)
-            arrived(0, 11, 12)
-            arrived(1, 11, 12)
-
-        @pl.when(step == 4)
-        def _():
-            for j in range(1, group):
-                tcopy(2, j).start()
-            forward_first(2)
-            first_phase(0)
-            arrived(2, 0)
-
-        @pl.when(step == 5)
-        def _():
-            forward_second(2)
-            arrived(2, 7, 8)
-
-        @pl.when(step == 6)
-        def _():
-            arrived(2, 9, 10)
-
-        @pl.when(step == 7)
-        def _():
-            second_phase(0)
-            forward_third(2)
-            arrived(2, 11, 12)
-
-        @pl.when(step < 4)
-        def _():
-            behind_block(step)
-
-        @pl.when(step >= 4)
-        def _():
-            ahead_block(step - 4)
-
-        for s in range(8):
-
-            @pl.when(step == s)
-            def _(s=s):
-                scopy(s // 4, s % 4).start()
-
-        return carry
-
-    lax.fori_loop(0, 8, stage, 0)
-    first_phase(1)
-
-    wrows = wgs[0]
-    for j in range(1, group):
-        tcopy(2, j).wait_recv()
-        wrows = wrows + wgr[j]
-    probs = ptab[0, 0]
-    logit_grad = probs * (wrows - jnp.sum(probs * wrows, axis=0, keepdims=True))
-    padded = jnp.concatenate([logit_grad, jnp.zeros((tokens - experts, tokens), f32)], axis=0)
-    lg_rows[...] = padded.T.astype(bf16)
-    gacc[...] = jnp.zeros_like(gacc)
 
     def total_rows(m, i):
         rows = pl.ds(i * small, small)
@@ -772,22 +693,112 @@
         zcopy(1, i).start()
 
     order = [side * SUB + q for q in range(SUB) for side in range(2)]
-    for i in order:
-        finish_behind(i)
-
-    second_phase(1)
-    factor = (tokens * group) ** (-0.5)
-    pad_rows = rgp.shape[1]
-    lg_short = padded[0:pad_rows, :].astype(bf16)
-    span = rgp.shape[2]
-    which = lax.broadcasted_iota(jnp.int32, (pad_rows, span), 0)
-    for d in range(group):
-        cols = slice(d * span, (d + 1) * span)
-        grads = jnp.dot(lg_short, gat[1, 0, 0:tokens, cols], preferred_element_type=f32)
-        rgp[d] = jnp.where(which == experts, gacc[:, cols], grads) * factor
-    for j in range(1, group):
-        tcopy(3, j).start()
-
+
+    def finish_all_behind():
+        wrows = wgs[0]
+        for j in range(1, group):
+            tcopy(2, j).wait_recv()
+            wrows = wrows + wgr[j]
+        probs = ptab[0, 0]
+        logit_grad = probs * (wrows - jnp.sum(probs * wrows, axis=0, keepdims=True))
+        padded = jnp.concatenate([logit_grad, jnp.zeros((tokens - experts, tokens), f32)], axis=0)
+        lg_rows[...] = padded.T.astype(bf16)
+        gacc[...] = jnp.zeros_like(gacc)
+
+        for i in order:
+            finish_behind(i)
+        factor = (tokens * group) ** (-0.5)
+        pad_rows = rgp.shape[1]
+        lg_short = padded[0:pad_rows, :].astype(bf16)
+        span = rgp.shape[2]
+        which = lax.broadcasted_iota(jnp.int32, (pad_rows, span), 0)
+        for d in range(group):
+            cols = slice(d * span, (d + 1) * span)
+            grads = jnp.dot(lg_short, gat[1, 0, 0:tokens, cols], preferred_element_type=f32)
+            rgp[d] = jnp.where(which == experts, gacc[:, cols], grads) * factor
+        for j in range(1, group):
+            tcopy(3, j).start()
+
+
+    forward_first(0)
+    forward_second(0)
+
+    def stage(step, carry):
+        @pl.when(step == 0)
+        def _():
+            arrived(0, 0)
+            arrived(1, 0)
+
+        @pl.when(step == 1)
+        def _():
+            forward_first(1)
+            forward_second(1)
+            for i in (1, 3, 2, 4, 0):
+                gcopy(2, i).start()
+            arrived(0, 7, 8)
+            arrived(1, 7, 8)
+
+        @pl.when(step == 2)
+        def _():
+            arrived(0, 9, 10)
+            arrived(1, 9, 10)
+            send_block(0, 0)
+
+        @pl.when(step == 3)
+        def _():
+            forward_third(0)
+            forward_third(1)
+            send_block(0, 1)
+            send_block(0, 2)
+            forward_first(2)
+            arrived(0, 11, 12)
+            arrived(1, 11, 12)
+
+        @pl.when(step == 4)
+        def _():
+            for j in range(1, group):
+                tcopy(2, j).start()
+            send_block(0, 3)
+            forward_second(2)
+            forward_third(2)
+            arrived(2, 11, 12)
+
+        @pl.when(step == 5)
+        def _():
+            send_block(1, 3)
+            arrived(2, 9, 10)
+
+        @pl.when(step == 6)
+        def _():
+            second_phase(0)
+            send_block(1, 2)
+            arrived(2, 7, 8)
+
+        @pl.when(step == 7)
+        def _():
+            send_block(1, 1)
+            arrived(2, 0)
+            second_phase(1)
+            finish_all_behind()
+
+        @pl.when(step < 4)
+        def _():
+            behind_block(step)
+
+        @pl.when(step >= 4)
+        def _():
+            ahead_block(7 - step)
+
+        for s in range(8):
+
+            @pl.when(step == s)
+            def _(s=s):
+                scopy(s // 4, s if s < 4 else 7 - s).start()
+
+        return carry
+
+    lax.fori_loop(0, 8, stage, 0)
+    send_block(1, 0)
     for i in order:
         finish_ahead(i)
 
@@ -811,6 +822,20 @@
                 xcopy(m, k, q).wait_send()
         for i in range(2 * SUB):
             zcopy(m, i).wait()
+
+
+def place_kernel(fwd_ref, back_ref, sums_ref, fwd_out, back_out, router_out, gain_out, sems):
+    experts = router_out.shape[0]
+    copies = [
+        pltpu.make_async_copy(fwd_ref, fwd_out, sems.at[0]),
+        pltpu.make_async_copy(back_ref, back_out, sems.at[1]),
+    ]
+    for copy in copies:
+        copy.start()
+    router_out[...] = sums_ref[0:experts, :]
+    gain_out[...] = sums_ref[experts : experts + 1, :]
+    for copy in copies:
+        copy.wait()
 
 
 def kernel_body(
@@ -840,7 +865,7 @@
     half = tokens // 2
     kv_width = cache_keys.shape[2]
     f32, bf16 = jnp.float32, jnp.bfloat16
-    table = jnp.pad(router[0].T, ((0, pad_experts - experts), (0, 0)))
+    table = router[0].T
     hbm = pl.BlockSpec(memory_space=pl.ANY)
     near = pl.BlockSpec(memory_space=pltpu.VMEM)
     copies = 13
@@ -931,7 +956,20 @@
         backward_ids[0].T,
         output_grad[0],
     )
-    return (out_fwd[None], out_back[None], sums[:experts].T[None], sums[experts][None])
+    span = width // group
+    out_fwd, out_back, router_part, gain_part = pl.pallas_call(
+        place_kernel,
+        out_shape=(
+            jax.ShapeDtypeStruct((tokens, width), bf16),
+            jax.ShapeDtypeStruct((tokens, width), bf16),
+            jax.ShapeDtypeStruct((experts, span), f32),
+            jax.ShapeDtypeStruct((1, span), f32),
+        ),
+        in_specs=[hbm, hbm, near],
+        out_specs=(hbm, hbm, near, near),
+        scratch_shapes=[dma((2,))],
+    )(out_fwd, out_back, sums)
+    return (out_fwd[None], out_back[None], router_part.T[None], gain_part)
 
 
 def body(*operands):

time: 133 us -> 154 us (1.16)
  Pallas kernels: 123 us -> 153 us
  local copies, waits for them, and re-layouts: 7.71 us -> 0 us
    pallas_call x0 -> x1, Pallas kernels: none -> 34.2 us  [kernel_body(): pl.pallas_call(place_kernel, out_shape=(jax.ShapeDtypeStruct((tokens, wid...]
    pallas_call x1, Pallas kernels: 123 us -> 118 us  [kernel_body(): pl.pallas_call(section_kernel, out_shape=(jax.ShapeDtypeStruct((tokens, w...]
    unnamed x2 -> x0, local copies, waits for them, and re-layouts: 3.76 us -> none
where the time goes in v1:
time: 154 us
  Pallas kernels  153 us (99%)
    pallas_call x1, Pallas kernels, kernel_body(): pl.pallas_call(section_kernel, out_shape=(jax.ShapeDtypeStruct((tokens, w...  118 us
    pallas_call x1, Pallas kernels, kernel_body(): pl.pallas_call(place_kernel, out_shape=(jax.ShapeDtypeStruct((tokens, wid...  34.2 us

profile of v1, /device:TPU:0, one launch (start us, length us, event | category | flops | bytes accessed | tf_op | source)
XLA Modules:
  0.0 154.0 jit_solution(11274503439882714892)
XLA Ops:
  1.3 118.5 %shard_map.183 = (bf16[128,2048]{1,0:T(8,128)(2,1)}, bf16[128,2048]{1,0:T(8,128)(2,1)}, f32[16,256]{1,0:T(8,128)}) custom-call(s32[1,1]{1,0:T(1,128)S(6)} %copy.20.length_ref, bf16[128,2048]{1,0:T(8,128)(2,1)} %bitcast.28, bf16[128,2048]{1,0:T(8,128)(2,1)} %bitcast.29, bf16[128,256]{1,0:T(8,128)(2,1)} %bitcast.32, bf16[128,256]{1,0:T(8,128)(2,1)} %bitcast.33, ...), custom_call_target="tpu_custom_call" | custom-call | tf_op jit(solution)/shard_map/pallas_call | solution.py:873
  119.8 34.2 %shard_map.184 = (bf16[128,2048]{1,0:T(8,128)(2,1)}, bf16[128,2048]{1,0:T(8,128)(2,1)}, f32[8,256]{1,0:T(8,128)}, f32[1,256]{1,0:T(1,128)}) custom-call(bf16[128,2048]{1,0:T(8,128)(2,1)} %get-tuple-element.11.fwd_ref, bf16[128,2048]{1,0:T(8,128)(2,1)} %get-tuple-element.12.back_ref, f32[16,256]{1,0:T(8,128)} %get-tuple-element.13.sums_ref), custom_call_target="tpu_custom_call" | custom-call | tf_op jit(solution)/shard_map/pallas_call | solution.py:960
